TPU v7x, 512 devices: a whole 4x4x16 slice. The times are simulated.
512 devices in a mesh: expert: 64 (over x, z), tensor: 8 (over y, core).
Axes of the slice: x: 4, y: 4, z: 16, core: 2. Of those that a mesh axis runs over, the one named last changes fastest.
Arguments:
- first_half: bfloat16 [8192, 2048], P('expert', 'tensor'), may hold values from -6 to 6
- second_half: bfloat16 [8192, 2048], P('expert', 'tensor'), may hold values from -1.5 to 1.5
- first_grad: bfloat16 [8192, 2048], P('expert', 'tensor'), may hold values from -1.5 to 1.5
- second_grad: bfloat16 [8192, 2048], P('expert', 'tensor'), may hold values from -6 to 6
- expert_ids: int32 [8192, 6], P('expert'), may hold values from 0 to 63, as said below
- gate_weights: bfloat16 [8192, 6], P('expert'), may hold values from 0.049804688 to 0.5
- expert_in: bfloat16 [64, 2, 1408, 2048], P('expert', None, 'tensor'), may hold values from -0.125 to 0.125
- expert_out: bfloat16 [64, 1408, 2048], P('expert', 'tensor'), may hold values from -0.15625 to 0.15625
Outputs:
- restored: bfloat16 [8192, 2048], P('expert', 'tensor')
- carried_grad: bfloat16 [8192, 2048], P('expert', 'tensor')
- gate_grad: float32 [8192, 6], P('expert')
- grad_in: bfloat16 [64, 2, 1408, 2048], P('expert', None, 'tensor')
- grad_out: bfloat16 [64, 1408, 2048], P('expert', 'tensor')
Inputs may be any that keep to these rules, and one draw needn't show every extreme that they name: `expert_ids`: each token names 6 different experts. In the rows of one index of expert (128 tokens) each expert is named by at least 10 and at most 14 tokens, and one expert is named by exactly 14 tokens of every index of expert.
All inputs are finite; a program needn't handle non-finite values.
Results may differ from a plain program's by a relative error of at most 0.02.
Values may be sent and summed in bfloat16 or wider, within the bound.
A program may use at most 128 MiB of HBM per device.

v0:
```python
import jax
import jax.numpy as jnp
from jax import lax
from jax.sharding import PartitionSpec as P


def expert_work(slot_rows, slot_cots, slot_gates, weights_in, weights_out):
    pre = jnp.einsum("erd,ekhd->ekrh", slot_rows, weights_in, preferred_element_type=jnp.float32)
    gate_pre = pre[:, 0]
    up_pre = pre[:, 1]
    sigma = jax.nn.sigmoid(gate_pre)
    active = gate_pre * sigma
    hidden = (active * up_pre).astype(jnp.bfloat16)
    part_out = jnp.einsum("erh,ehd->erd", hidden, weights_out, preferred_element_type=jnp.float32)
    gate_piece = jnp.sum(slot_cots.astype(jnp.float32) * part_out, axis=2)
    scaled = (slot_gates[:, :, None].astype(jnp.float32) * slot_cots.astype(jnp.float32)).astype(
        jnp.bfloat16
    )
    hidden_grad = jnp.einsum(
        "erd,ehd->erh", scaled, weights_out, preferred_element_type=jnp.float32
    )
    gate_pre_grad = (hidden_grad * up_pre * sigma * (1.0 + gate_pre * (1.0 - sigma))).astype(
        jnp.bfloat16
    )
    up_grad = (hidden_grad * active).astype(jnp.bfloat16)
    input_piece = jnp.einsum(
        "erh,ehd->erd", gate_pre_grad, weights_in[:, 0], preferred_element_type=jnp.float32
    ) + jnp.einsum("erh,ehd->erd", up_grad, weights_in[:, 1], preferred_element_type=jnp.float32)
    grad_gate = jnp.einsum(
        "erh,erd->ehd", gate_pre_grad, slot_rows, preferred_element_type=jnp.float32
    ).astype(jnp.bfloat16)
    grad_up = jnp.einsum(
        "erh,erd->ehd", up_grad, slot_rows, preferred_element_type=jnp.float32
    ).astype(jnp.bfloat16)
    grad_in = jnp.stack([grad_gate, grad_up], axis=1)
    grad_out = jnp.einsum(
        "erh,erd->ehd", hidden, scaled, preferred_element_type=jnp.float32
    ).astype(jnp.bfloat16)
    return (part_out, input_piece, gate_piece, grad_in, grad_out)


def body(
    first_half,
    second_half,
    first_grad,
    second_grad,
    expert_ids,
    gate_weights,
    expert_in,
    expert_out,
):
    tokens_here = expert_ids.shape[0]
    picks = expert_ids.shape[1]
    groups = lax.axis_size("expert")
    local_count = expert_in.shape[0]
    experts_all = groups * local_count
    capacity = tokens_here * picks * 7 // (6 * experts_all)
    routes = expert_ids.reshape(-1)
    onehot = (routes[:, None] == jnp.arange(experts_all, dtype=jnp.int32)[None, :]).astype(
        jnp.int32
    )
    before = jnp.cumsum(onehot, axis=0) - onehot
    slot_index = jnp.sum(before * onehot, axis=1)
    destination = routes * capacity + slot_index
    route_token = jnp.arange(tokens_here * picks, dtype=jnp.int32) // picks
    slot_token = (
        jnp.full((experts_all * capacity,), tokens_here, jnp.int32).at[destination].set(route_token)
    )
    slot_gate = (
        jnp.zeros((experts_all * capacity,), jnp.bfloat16)
        .at[destination]
        .set(gate_weights.reshape(-1))
    )
    slot_gate = slot_gate.reshape(experts_all, capacity)

    def to_slots(values):
        padded = jnp.concatenate([values, jnp.zeros((1, values.shape[1]), values.dtype)], axis=0)
        return padded[slot_token].reshape(experts_all, capacity, values.shape[1])

    def to_local(values):
        shaped = values.reshape((groups, local_count) + values.shape[1:])
        shaped = jnp.moveaxis(shaped, 1, 0)
        return shaped.reshape((local_count, groups * capacity) + values.shape[2:])

    def to_sources(values):
        shaped = values.reshape((local_count, groups, capacity) + values.shape[2:])
        shaped = jnp.moveaxis(shaped, 0, 1)
        return shaped.reshape((experts_all, capacity) + values.shape[2:])

    whole_first, whole_cots = (
        lax.all_gather(first_half, "tensor", axis=1, tiled=True),
        lax.all_gather(second_grad, "tensor", axis=1, tiled=True),
    )
    recv_rows, recv_cots, recv_gates = (
        lax.all_to_all(to_slots(whole_first), "expert", split_axis=0, concat_axis=0, tiled=True),
        lax.all_to_all(to_slots(whole_cots), "expert", split_axis=0, concat_axis=0, tiled=True),
        lax.all_to_all(slot_gate, "expert", split_axis=0, concat_axis=0, tiled=True),
    )
    results = expert_work(
        to_local(recv_rows), to_local(recv_cots), to_local(recv_gates), expert_in, expert_out
    )
    grad_in = results[3]
    grad_out = results[4]
    gate_all = to_sources(results[2]).astype(jnp.bfloat16)
    weights_f = gate_weights.astype(jnp.float32)
    out_all = to_sources(results[0].astype(jnp.bfloat16))
    input_all = to_sources(results[1].astype(jnp.bfloat16))
    back_out, back_input, back_gate = (
        lax.all_to_all(out_all, "expert", split_axis=0, concat_axis=0, tiled=True),
        lax.all_to_all(input_all, "expert", split_axis=0, concat_axis=0, tiled=True),
        lax.all_to_all(gate_all, "expert", split_axis=0, concat_axis=0, tiled=True),
    )
    width = back_out.shape[2]
    picked_out = back_out.reshape(-1, width)[destination].reshape(tokens_here, picks, width)
    picked_input = back_input.reshape(-1, width)[destination].reshape(tokens_here, picks, width)
    mixed = jnp.sum(weights_f[:, :, None] * picked_out.astype(jnp.float32), axis=1)
    summed_input = jnp.sum(picked_input.astype(jnp.float32), axis=1)
    branch_cols, input_cols = (
        lax.psum_scatter(
            mixed.astype(jnp.bfloat16), "tensor", scatter_dimension=1, tiled=True
        ).astype(jnp.float32),
        lax.psum_scatter(
            summed_input.astype(jnp.bfloat16), "tensor", scatter_dimension=1, tiled=True
        ).astype(jnp.float32),
    )
    gate_back = back_gate.astype(jnp.float32)
    gate_parts = gate_back.reshape(-1)[destination].reshape(tokens_here, picks)
    gate_grad = lax.psum(gate_parts, "tensor")
    restored = (second_half.astype(jnp.float32) - branch_cols).astype(jnp.bfloat16)
    carried_grad = (first_grad.astype(jnp.float32) + input_cols).astype(jnp.bfloat16)
    return (restored, carried_grad, gate_grad, grad_in, grad_out)


def solution(mesh):
    in_specs = (
        P("expert", "tensor"),
        P("expert", "tensor"),
        P("expert", "tensor"),
        P("expert", "tensor"),
        P("expert", None),
        P("expert", None),
        P("expert", None, "tensor", None),
        P("expert", "tensor", None),
    )
    out_specs = (
        P("expert", "tensor"),
        P("expert", "tensor"),
        P("expert", None),
        P("expert", None, "tensor", None),
        P("expert", "tensor", None),
    )
    return jax.shard_map(body, mesh=mesh, in_specs=in_specs, out_specs=out_specs, check_vma=False)
```

profile of v0, /device:TPU:1, one launch (start us, length us, event | category | flops | bytes accessed | tf_op | source)
XLA Modules:
  0.0 957.3 jit_solution(17557005658640460501)
XLA Ops:
  15.0 20.0 %all_gather.6 = bf16[128,2048]{1,0:T(8,128)(2,1)S(1)} all-gather(bf16[128,256]{1,0:T(8,128)(2,1)} %param.8), channel_id=1, replica_groups=mesh['expert'=64,'tensor'=8] {'tensor'}, dimensions={1}, use_global_device_ids=true | all-gather | bytes 589824 | tf_op jit(solution)/shard_map/all_gather | solution.py:91
  46.1 13.8 %all-to-all-start = ((bf16[64,14,2048]{2,1,0:T(8,128)(2,1)}), bf16[64,14,2048]{2,1,0:T(8,128)(2,1)}, u32[]{:S(2)}, u32[]{:S(2)}) async-start(bf16[64,14,2048]{2,1,0:T(8,128)(2,1)} %reshape.268), calls=%async_computation | async-start | bytes 8388608 | tf_op jit(solution)/shard_map/all_to_all | solution.py:95
  59.9 13.4 %all_gather.7 = bf16[128,2048]{1,0:T(8,128)(2,1)S(1)} all-gather(bf16[128,256]{1,0:T(8,128)(2,1)S(1)} %copy-done.4), channel_id=1, replica_groups=mesh['expert'=64,'tensor'=8] {'tensor'}, dimensions={1}, use_global_device_ids=true | all-gather | bytes 589824 | tf_op jit(solution)/shard_map/all_gather | solution.py:92
  84.4 159.6 %all-to-all-done = bf16[64,14,2048]{2,1,0:T(8,128)(2,1)} async-done(((bf16[64,14,2048]{2,1,0:T(8,128)(2,1)}), bf16[64,14,2048]{2,1,0:T(8,128)(2,1)}, u32[]{:S(2)}, u32[]{:S(2)}) %all-to-all-start) | async-done | bytes 3670048 | tf_op jit(solution)/shard_map/all_to_all | solution.py:95
  244.0 11.7 %all-to-all-start.3 = ((bf16[64,14,2048]{2,1,0:T(8,128)(2,1)}), bf16[64,14,2048]{2,1,0:T(8,128)(2,1)}, u32[]{:S(2)}, u32[]{:S(2)}) async-start(bf16[64,14,2048]{2,1,0:T(8,128)(2,1)} %reshape.274), calls=%async_computation.4 | async-start | bytes 8388608 | tf_op jit(solution)/shard_map/all_to_all | solution.py:96
  256.1 8.6 scatter_custom_fusion.1
  265.5 6.1 reshape.343
  276.5 161.1 %all-to-all-done.3 = bf16[64,14,2048]{2,1,0:T(8,128)(2,1)} async-done(((bf16[64,14,2048]{2,1,0:T(8,128)(2,1)}), bf16[64,14,2048]{2,1,0:T(8,128)(2,1)}, u32[]{:S(2)}, u32[]{:S(2)}) %all-to-all-start.3) | async-done | bytes 3670048 | tf_op jit(solution)/shard_map/all_to_all | solution.py:96
  437.6 13.3 %all-to-all-start.2 = ((bf16[64,1,14]{2,1,0:T(2,128)(2,1)}), bf16[64,1,14]{2,1,0:T(2,128)(2,1)S(1)}, u32[]{:S(2)}, u32[]{:S(2)}) async-start(bf16[64,1,14]{2,1,0:T(2,128)(2,1)} %all_to_all.29), calls=%async_computation.3 | async-start | bytes 65536 | tf_op jit(solution)/shard_map/all_to_all | solution.py:97
  450.9 6.5 reshape.283
  457.4 6.1 multiply_reduce_fusion.1
  469.6 15.0 %all-to-all-start.1 = ((bf16[64,14,2048]{2,1,0:T(8,128)(2,1)}), bf16[64,14,2048]{2,1,0:T(8,128)(2,1)}, u32[]{:S(2)}, u32[]{:S(2)}) async-start(bf16[64,14,2048]{2,1,0:T(8,128)(2,1)} %reshape_transpose_reshape.4), calls=%async_computation.1 | async-start | bytes 8388608 | tf_op jit(solution)/shard_map/all_to_all | solution.py:109
  484.8 6.4 reshape.282
  506.4 159.4 %all-to-all-done.1 = bf16[64,14,2048]{2,1,0:T(8,128)(2,1)} async-done(((bf16[64,14,2048]{2,1,0:T(8,128)(2,1)}), bf16[64,14,2048]{2,1,0:T(8,128)(2,1)}, u32[]{:S(2)}, u32[]{:S(2)}) %all-to-all-start.1) | async-done | bytes 3670048 | tf_op jit(solution)/shard_map/all_to_all | solution.py:109
  665.7 14.4 %all-to-all-start.4 = ((bf16[64,14,2048]{2,1,0:T(8,128)(2,1)}), bf16[64,14,2048]{2,1,0:T(8,128)(2,1)}, u32[]{:S(2)}, u32[]{:S(2)}) async-start(bf16[64,14,2048]{2,1,0:T(8,128)(2,1)} %reshape_transpose_reshape.10), calls=%async_computation.5 | async-start | bytes 8388608 | tf_op jit(solution)/shard_map/all_to_all | solution.py:110
  686.3 9.6 %gather_fusion.1 = bf16[768,2048]{1,0:T(8,128)(2,1)} fusion(bf16[896,2048]{1,0:T(8,128)(2,1)} %reshape.272, s32[1024]{0:T(1024)S(1)} %pad_clamp_fusion), kind=kCustom, calls=%fused_computation.1 | custom fusion | bytes 6294528 | tf_op jit(solution)/shard_map/gather | solution.py:114
  695.9 6.6 reshape.280
  702.5 7.4 multiply_reduce_fusion
  719.1 143.4 %all-to-all-done.4 = bf16[64,14,2048]{2,1,0:T(8,128)(2,1)} async-done(((bf16[64,14,2048]{2,1,0:T(8,128)(2,1)}), bf16[64,14,2048]{2,1,0:T(8,128)(2,1)}, u32[]{:S(2)}, u32[]{:S(2)}) %all-to-all-start.4) | async-done | bytes 3670048 | tf_op jit(solution)/shard_map/all_to_all | solution.py:110
  868.5 9.7 %gather_fusion.3 = bf16[768,2048]{1,0:T(8,128)(2,1)} fusion(bf16[896,2048]{1,0:T(8,128)(2,1)} %reshape.277, s32[1024]{0:T(1024)S(1)} %pad_clamp_fusion), kind=kCustom, calls=%fused_computation.3 | custom fusion | bytes 6294528 | tf_op jit(solution)/shard_map/gather | solution.py:115
  878.2 6.3 reshape.278
  893.9 12.6 %all-to-all-start.5 = ((bf16[64,1,14]{2,1,0:T(2,128)(2,1)}), bf16[64,1,14]{2,1,0:T(2,128)(2,1)S(1)}, u32[]{:S(2)}, u32[]{:S(2)}) async-start(bf16[64,1,14]{2,1,0:T(2,128)(2,1)} %convert_element_type.209), calls=%async_computation.7 | async-start | bytes 65536 | tf_op jit(solution)/shard_map/all_to_all | solution.py:111
  912.8 6.9 all-to-all-done.5
  923.3 23.2 %psum.7 = f32[128,6]{1,0:T(8,128)S(1)} all-reduce(f32[128,6]{1,0:T(8,128)S(1)} %reshape.279), channel_id=1, replica_groups=mesh['expert'=64,'tensor'=8] {'tensor'}, use_global_device_ids=true, to_apply=%region_10.11 | all-reduce | flops 768 | bytes 6144 | tf_op jit(solution)/shard_map/psum | solution.py:128
  (75 shorter events, 101.6 us)
Async XLA Ops:
  7.2 450.3 %copy-start = (bf16[1,176,2048]{2,1,0:T(8,128)(2,1)S(1)}, bf16[1,176,2048]{2,1,0:T(8,128)(2,1)}, u32[]{:S(2)}) copy-start(bf16[1,176,2048]{2,1,0:T(8,128)(2,1)} %param.15) | copy-start | bytes 2162692
  46.1 13.8 %copy-start.4 = (bf16[128,256]{1,0:T(8,128)(2,1)S(1)}, bf16[128,256]{1,0:T(8,128)(2,1)}, u32[]{:S(2)}) copy-start(bf16[128,256]{1,0:T(8,128)(2,1)} %param.11) | copy-start | bytes 196612
  46.1 197.9 %all-to-all-start = ((bf16[64,14,2048]{2,1,0:T(8,128)(2,1)}), bf16[64,14,2048]{2,1,0:T(8,128)(2,1)}, u32[]{:S(2)}, u32[]{:S(2)}) async-start(bf16[64,14,2048]{2,1,0:T(8,128)(2,1)} %reshape.268), calls=%async_computation | async-start | bytes 8388608 | tf_op jit(solution)/shard_map/all_to_all | solution.py:95
  84.4 171.3 %copy-start.7 = (bf16[128,6]{0,1:T(8,128)(2,1)S(1)}, bf16[128,6]{0,1:T(8,128)(2,1)}, u32[]{:S(2)}) copy-start(bf16[128,6]{0,1:T(8,128)(2,1)} %param.13) | copy-start | bytes 4612
  244.0 193.6 %all-to-all-start.3 = ((bf16[64,14,2048]{2,1,0:T(8,128)(2,1)}), bf16[64,14,2048]{2,1,0:T(8,128)(2,1)}, u32[]{:S(2)}, u32[]{:S(2)}) async-start(bf16[64,14,2048]{2,1,0:T(8,128)(2,1)} %reshape.274), calls=%async_computation.4 | async-start | bytes 8388608 | tf_op jit(solution)/shard_map/all_to_all | solution.py:96
  265.5 6.1 copy-start.2
  275.3 1.0 copy-start.3
  437.6 32.0 %all-to-all-start.2 = ((bf16[64,1,14]{2,1,0:T(2,128)(2,1)}), bf16[64,1,14]{2,1,0:T(2,128)(2,1)S(1)}, u32[]{:S(2)}, u32[]{:S(2)}) async-start(bf16[64,1,14]{2,1,0:T(2,128)(2,1)} %all_to_all.29), calls=%async_computation.3 | async-start | bytes 65536 | tf_op jit(solution)/shard_map/all_to_all | solution.py:97
  469.6 196.2 %all-to-all-start.1 = ((bf16[64,14,2048]{2,1,0:T(8,128)(2,1)}), bf16[64,14,2048]{2,1,0:T(8,128)(2,1)}, u32[]{:S(2)}, u32[]{:S(2)}) async-start(bf16[64,14,2048]{2,1,0:T(8,128)(2,1)} %reshape_transpose_reshape.4), calls=%async_computation.1 | async-start | bytes 8388608 | tf_op jit(solution)/shard_map/all_to_all | solution.py:109
  665.7 196.8 %all-to-all-start.4 = ((bf16[64,14,2048]{2,1,0:T(8,128)(2,1)}), bf16[64,14,2048]{2,1,0:T(8,128)(2,1)}, u32[]{:S(2)}, u32[]{:S(2)}) async-start(bf16[64,14,2048]{2,1,0:T(8,128)(2,1)} %reshape_transpose_reshape.10), calls=%async_computation.5 | async-start | bytes 8388608 | tf_op jit(solution)/shard_map/all_to_all | solution.py:110
  680.1 267.1 %reduce-scatter.3.cloned.1.call-start = ((), (), s32[]{:S(2)}) async-start(), calls=%async_computation.8 | async-start | bytes 589824 | tf_op jit(solution)/shard_map/reduce_scatter | solution.py:119
  709.9 238.8 %reduce-scatter.5.cloned.1.call-start = ((), (), s32[]{:S(2)}) async-start(), calls=%async_computation.9 | async-start | bytes 589824 | tf_op jit(solution)/shard_map/reduce_scatter | solution.py:122
  893.9 25.8 %all-to-all-start.5 = ((bf16[64,1,14]{2,1,0:T(2,128)(2,1)}), bf16[64,1,14]{2,1,0:T(2,128)(2,1)S(1)}, u32[]{:S(2)}, u32[]{:S(2)}) async-start(bf16[64,1,14]{2,1,0:T(2,128)(2,1)} %convert_element_type.209), calls=%async_computation.7 | async-start | bytes 65536 | tf_op jit(solution)/shard_map/all_to_all | solution.py:111
  906.5 43.7 %copy-start.1 = (bf16[1,176,2048]{2,1,0:T(8,128)(2,1)S(1)}, bf16[1,176,2048]{2,1,0:T(8,128)(2,1)}, u32[]{:S(2)}) copy-start(bf16[1,176,2048]{2,1,0:T(8,128)(2,1)} %param.15) | copy-start | bytes 2162692
  911.6 35.6 %copy-start.5 = (bf16[128,256]{1,0:T(8,128)(2,1)S(1)}, bf16[128,256]{1,0:T(8,128)(2,1)}, u32[]{:S(2)}) copy-start(bf16[128,256]{1,0:T(8,128)(2,1)} %param.9) | copy-start | bytes 196612
  911.6 37.1 %copy-start.6 = (bf16[128,256]{1,0:T(8,128)(2,1)S(1)}, bf16[128,256]{1,0:T(8,128)(2,1)}, u32[]{:S(2)}) copy-start(bf16[128,256]{1,0:T(8,128)(2,1)} %param.10) | copy-start | bytes 196612
Sparse Core Ops, SparseCore 0:
  710.0 38.4 reduce-scatter.2
  890.3 35.8 reduce-scatter.4
where the time goes:
time: 967 us; the launch traced here: 957 us
  waiting for transfers between devices  630 us (65%)
  local copies, waits for them, and re-layouts  124 us (13%)
  starting transfers between devices  81.2 us (8%)
  blocking collectives  56.7 us (6%)
  matrix products  30 us (3%)
  other arithmetic  20.4 us (2%)
  between operations  14.5 us (1%)
    all_to_all x1, waiting for transfers between devices, body(): lax.all_to_all(to_slots(whole_cots), 'expert', split_axis=0, concat_axis=...  161 us
    all_to_all x1, waiting for transfers between devices, body(): lax.all_to_all(to_slots(whole_first), 'expert', split_axis=0, concat_axis...  160 us
    all_to_all x1, waiting for transfers between devices, body(): lax.all_to_all(out_all, 'expert', split_axis=0, concat_axis=0, tiled=True)  159 us
    all_to_all x1, waiting for transfers between devices, body(): lax.all_to_all(input_all, 'expert', split_axis=0, concat_axis=0, tiled=True)  143 us
    psum x1, blocking collectives, body(): gate_grad = lax.psum(gate_parts, 'tensor')  23.2 us
    all_gather x1, blocking collectives, body(): lax.all_gather(first_half, 'tensor', axis=1, tiled=True)  20 us
  transfers between devices with their start and end apart: 8, of which 5 were waited for; matrix products, arithmetic and copies ran while one was open for 16% of the time, Pallas kernels for 0%

commit v1 on v0

v1 whole, which is shorter than its diff:
```python
import jax
import jax.numpy as jnp
from jax import lax
from jax.sharding import PartitionSpec as P

F32, BF16 = jnp.float32, jnp.bfloat16


def body(
    first_half,
    second_half,
    first_grad,
    second_grad,
    expert_ids,
    gate_weights,
    expert_in,
    expert_out,
):
    tokens, picks = expert_ids.shape
    experts = lax.axis_size("expert")
    cap = tokens * picks * 7 // (6 * experts)
    columns = first_half.shape[1]
    hits = expert_ids[:, :, None] == jnp.arange(experts, dtype=jnp.int32)
    member = jnp.any(hits, axis=1)
    gate = jnp.sum(jnp.where(hits, gate_weights.astype(F32)[:, :, None], 0.0), axis=1)
    below = (jnp.arange(tokens)[:, None] > jnp.arange(tokens)[None, :]).astype(BF16)
    rank = jnp.dot(below, member.astype(BF16), preferred_element_type=F32)
    slot = jnp.arange(cap, dtype=F32)
    chosen = member.T[:, None, :] & (rank.T[:, None, :] == slot[None, :, None])
    pick = chosen.astype(BF16).reshape(experts * cap, tokens)
    weigh = jnp.where(chosen, gate.T[:, None, :], 0.0).astype(BF16)
    weigh = weigh.reshape(experts * cap, tokens)

    def over(values):
        shaped = values.reshape(experts, cap, columns)
        moved = lax.all_to_all(shaped, "expert", split_axis=0, concat_axis=0, tiled=True)
        return moved.reshape(experts * cap, columns)

    rows = jnp.dot(pick, first_half, preferred_element_type=F32).astype(BF16)
    scaled_mine = jnp.dot(weigh, second_grad, preferred_element_type=F32).astype(BF16)
    rows_all = lax.all_gather(over(rows), "tensor", axis=1, tiled=True)
    scaled = lax.all_gather(over(scaled_mine), "tensor", axis=1, tiled=True)
    w_gate, w_up, w_down = expert_in[0, 0], expert_in[0, 1], expert_out[0]

    def mm(spec, a, b):
        return jnp.einsum(spec, a, b, preferred_element_type=F32)

    gate_pre = mm("rd,hd->rh", rows_all, w_gate)
    up_pre = mm("rd,hd->rh", rows_all, w_up)
    sigma = jax.nn.sigmoid(gate_pre)
    active = gate_pre * sigma
    hidden = (active * up_pre).astype(BF16)
    part_out = mm("rh,hd->rd", hidden, w_down).astype(BF16)
    hidden_grad = mm("rd,hd->rh", scaled, w_down)
    gate_pre_grad = (hidden_grad * up_pre * sigma * (1.0 + gate_pre * (1.0 - sigma))).astype(BF16)
    up_grad = (hidden_grad * active).astype(BF16)
    input_piece = (mm("rh,hd->rd", gate_pre_grad, w_gate) + mm("rh,hd->rd", up_grad, w_up)).astype(BF16)
    out_mine = lax.psum_scatter(part_out, "tensor", scatter_dimension=1, tiled=True)
    input_mine = lax.psum_scatter(input_piece, "tensor", scatter_dimension=1, tiled=True)
    grad_gate = mm("rh,rd->hd", gate_pre_grad, rows_all).astype(BF16)
    grad_up = mm("rh,rd->hd", up_grad, rows_all).astype(BF16)
    grad_out = mm("rh,rd->hd", hidden, scaled).astype(BF16)
    back_out, back_input = over(out_mine), over(input_mine)
    branch = mm("st,sd->td", weigh, back_out)
    branch_grad = mm("st,sd->td", pick, back_input)
    dots = jnp.sum(scaled_mine.astype(F32) * back_out.astype(F32), axis=1)
    table = jnp.sum(jnp.where(chosen, dots.reshape(experts, cap, 1), 0.0), axis=1).T
    parts = jnp.sum(jnp.where(hits, table[:, None, :], 0.0), axis=2) / gate_weights.astype(F32)
    gate_grad = lax.psum(parts, "tensor")
    restored = (second_half.astype(F32) - branch).astype(BF16)
    carried_grad = (first_grad.astype(F32) + branch_grad).astype(BF16)
    return (restored, carried_grad, gate_grad, jnp.stack([grad_gate, grad_up])[None], grad_out[None])


def solution(mesh):
    tokens = P("expert", "tensor")
    routes = P("expert", None)
    weights = (P("expert", None, "tensor", None), P("expert", "tensor", None))
    return jax.shard_map(
        body,
        mesh=mesh,
        in_specs=(tokens, tokens, tokens, tokens, routes, routes, *weights),
        out_specs=(tokens, tokens, routes, *weights),
        check_vma=False,
    )
```

time: 967 us -> 296 us (0.31)
  the two profiles are of different devices: /device:TPU:1 before, /device:TPU:31 now
where the time goes in v1:
time: 296 us
  waiting for transfers between devices  115 us (39%)
  blocking collectives  98.2 us (33%)
  starting transfers between devices  30.5 us (10%)
  matrix products  29.1 us (10%)
  between operations  14.1 us (5%)
  local copies, waits for them, and re-layouts  6.76 us (2%)
    all_to_all x2, blocking collectives, over(): lax.all_to_all(shaped, 'expert', split_axis=0, concat_axis=0, tiled=True)  84.9 us
    reduce_scatter x1, waiting for transfers between devices, body(): lax.psum_scatter(part_out, 'tensor', scatter_dimension=1, tiled=True)  39.9 us
    all_gather x1, waiting for transfers between devices, body(): scaled = lax.all_gather(over(scaled_mine), 'tensor', axis=1, tiled=True)  35.3 us
    all_to_all x2, starting transfers between devices, over(): lax.all_to_all(shaped, 'expert', split_axis=0, concat_axis=0, tiled=True)  30.3 us
    reduce_scatter x1, waiting for transfers between devices, body(): lax.psum_scatter(input_piece, 'tensor', scatter_dimension=1, tiled=True)  29.5 us
    dot_general x11, matrix products, mm(): return jnp.einsum(spec, a, b, preferred_element_type=F32)  27.6 us
    psum x1, blocking collectives, body(): gate_grad = lax.psum(parts, 'tensor')  13.3 us
    all_to_all x2, waiting for transfers between devices, over(): lax.all_to_all(shaped, 'expert', split_axis=0, concat_axis=0, tiled=True)  9.82 us
  transfers between devices with their start and end apart: 6, of which 5 were waited for; matrix products, arithmetic and copies ran while one was open for 9% of the time, Pallas kernels for 0%

profile of v1, /device:TPU:31, one launch (start us, length us, event | category | flops | bytes accessed | tf_op | source)
XLA Modules:
  0.0 295.9 jit_solution(14118723173858887704)
XLA Ops:
  8.8 1.1 convolution_convert_fusion.5
  10.0 47.3 %all_to_all.20 = bf16[64,14,256]{2,1,0:T(8,128)(2,1)S(1)} all-to-all(bf16[64,14,256]{2,1,0:T(8,128)(2,1)S(1)} %reshape.49), channel_id=1, replica_groups=mesh['expert'=64,'tensor'=8] {'expert'}, dimensions={0} | all-to-all | bytes 917504 | tf_op jit(solution)/shard_map/all_to_all | solution.py:36
  58.9 37.7 %all_to_all.21 = bf16[64,14,256]{2,1,0:T(8,128)(2,1)S(1)} all-to-all(bf16[64,14,256]{2,1,0:T(8,128)(2,1)S(1)} %reshape.52), channel_id=1, replica_groups=mesh['expert'=64,'tensor'=8] {'expert'}, dimensions={0} | all-to-all | bytes 917504 | tf_op jit(solution)/shard_map/all_to_all | solution.py:36
  97.5 4.5 %fusion.11 = f32[896,176]{0,1:T(8,128)} fusion(bf16[896,2048]{1,0:T(8,128)(2,1)} %all-gather.3.cloned.1.call-done, bf16[1,2,176,2048]{3,2,1,0:T(8,128)(2,1)} %param.14), kind=kOutput, calls=%fused_computation.22 | convolution fusion | flops 645922816 | bytes 5021696 | tf_op jit(solution)/shard_map/rd,hd->rh/dot_general | solution.py:46
  102.1 2.2 fusion.15
  104.3 35.3 %all-gather.5.cloned.1.call-done = bf16[896,2048]{1,0:T(8,128)(2,1)} async-done(((bf16[896,256]{1,0:T(8,128)(2,1)}), bf16[896,2048]{1,0:T(8,128)(2,1)}) %all-gather.5.cloned.1.call-update) | async-done | bytes 3670032 | tf_op jit(solution)/shard_map/all_gather | solution.py:42
  139.6 4.5 %multiply_convert_fusion = (bf16[896,176]{0,1:T(8,128)(2,1)}, bf16[896,176]{0,1:T(8,128)(2,1)S(1)}, bf16[896,176]{0,1:T(8,128)(2,1)S(1)}) fusion(f32[896,176]{0,1:T(8,128)} %fusion.15, f32[896,176]{0,1:T(8,128)} %fusion.11, bf16[896,2048]{1,0:T(8,128)(2,1)} %all-gather.5.cloned.1.call-done, bf16[1,176,2048]{2,1,0:T(8,128)(2,1)S(1)} %copy-done), kind=kOutput, calls=%fused_computation.32 | convolution fusion | flops 648288256 | bytes 6598656 | tf_op jit(solution)/shard_map/rd,hd->rh/dot_general | solution.py:46
  144.1 3.1 %convolution_convert_fusion = bf16[896,2048]{1,0:T(8,128)(2,1)} fusion(bf16[896,176]{0,1:T(8,128)(2,1)S(1)} %get-tuple-element.7, bf16[1,176,2048]{2,1,0:T(8,128)(2,1)S(1)} %copy-done), kind=kOutput, calls=%fused_computation.1 | convolution fusion | flops 647757824 | bytes 4706304 | tf_op jit(solution)/shard_map/rh,hd->rd/dot_general | solution.py:46
  147.3 1.2 fusion.13
  148.5 3.1 %add_convert_fusion = bf16[896,2048]{1,0:T(8,128)(2,1)} fusion(f32[896,2048]{1,0:T(8,128)S(1)} %fusion.13, bf16[896,176]{0,1:T(8,128)(2,1)S(1)} %copy-done.5, bf16[1,2,176,2048]{3,2,1,0:T(8,128)(2,1)S(1)} %copy-done.4), kind=kOutput, calls=%fused_computation | convolution fusion | flops 649592832 | bytes 12046336 | tf_op jit(solution)/shard_map/rh,hd->rd/dot_general | solution.py:46
  151.6 39.9 %reduce-scatter.3.cloned.1.call-done = bf16[896,256]{1,0:T(8,128)(2,1)} async-done(((bf16[896,2048]{1,0:T(8,128)(2,1)}), bf16[896,256]{1,0:T(8,128)(2,1)}) %reduce-scatter.3.cloned.1.call-update) | async-done | bytes 458768 | tf_op jit(solution)/shard_map/reduce_scatter | solution.py:58
  191.5 1.9 reshape.51
  193.4 15.3 %all-to-all-start.1 = ((bf16[64,14,256]{2,1,0:T(8,128)(2,1)}), bf16[64,14,256]{2,1,0:T(8,128)(2,1)S(1)}, u32[]{:S(2)}, u32[]{:S(2)}) async-start(bf16[64,14,256]{2,1,0:T(8,128)(2,1)} %reshape.51), calls=%async_computation.2 | async-start | bytes 1048576 | tf_op jit(solution)/shard_map/all_to_all | solution.py:36
  208.8 29.5 %reduce-scatter.5.cloned.1.call-done = bf16[896,256]{1,0:T(8,128)(2,1)} async-done(((bf16[896,2048]{1,0:T(8,128)(2,1)}), bf16[896,256]{1,0:T(8,128)(2,1)}) %reduce-scatter.5.cloned.1.call-update) | async-done | bytes 458768 | tf_op jit(solution)/shard_map/reduce_scatter | solution.py:59
  238.3 1.9 reshape.54
  240.6 15.0 %all-to-all-start.3 = ((bf16[64,14,256]{2,1,0:T(8,128)(2,1)}), bf16[64,14,256]{2,1,0:T(8,128)(2,1)}, u32[]{:S(2)}, u32[]{:S(2)}) async-start(bf16[64,14,256]{2,1,0:T(8,128)(2,1)} %reshape.54), calls=%async_computation.5 | async-start | bytes 1048576 | tf_op jit(solution)/shard_map/all_to_all | solution.py:36
  255.6 3.1 %fusion.1 = bf16[1,176,2048]{2,1,0:T(8,128)(2,1)S(1)} fusion(bf16[896,176]{0,1:T(8,128)(2,1)S(1)} %copy-done.6, bf16[896,2048]{1,0:T(8,128)(2,1)} %all-gather.3.cloned.1.call-done), kind=kOutput, calls=%fused_computation.6 | convolution fusion | flops 646283264 | bytes 4706304 | tf_op jit(solution)/shard_map/rh,rd->hd/dot_general | solution.py:46
  258.8 0.9 fusion
  259.7 1.2 maximum_bitcast_fusion
  261.0 1.8 fusion.2
  263.6 13.3 %psum.7 = f32[128,6]{0,1:T(8,128)} all-reduce(f32[128,6]{0,1:T(8,128)S(1)} %convert_divide_fusion), channel_id=1, replica_groups=mesh['expert'=64,'tensor'=8] {'tensor'}, use_global_device_ids=true, to_apply=%region_7.8 | all-reduce | flops 768 | bytes 6144 | tf_op jit(solution)/shard_map/psum | solution.py:69
  276.9 1.0 fusion.6
  277.9 9.4 %all-to-all-done.3 = bf16[64,14,256]{2,1,0:T(8,128)(2,1)} async-done(((bf16[64,14,256]{2,1,0:T(8,128)(2,1)}), bf16[64,14,256]{2,1,0:T(8,128)(2,1)}, u32[]{:S(2)}, u32[]{:S(2)}) %all-to-all-start.3) | async-done | bytes 458784 | tf_op jit(solution)/shard_map/all_to_all | solution.py:36
  287.3 2.0 fusion.5
  (59 shorter events, 5.4 us)
Async XLA Ops:
  7.2 132.5 %copy-start = (bf16[1,176,2048]{2,1,0:T(8,128)(2,1)S(1)}, bf16[1,176,2048]{2,1,0:T(8,128)(2,1)}, u32[]{:S(2)}) copy-start(bf16[1,176,2048]{2,1,0:T(8,128)(2,1)} %param.15) | copy-start | bytes 2162692
  7.2 51.1 %copy-start.8 = (s32[128,6]{0,1:T(8,128)S(1)}, s32[128,6]{0,1:T(8,128)}, u32[]{:S(2)}) copy-start(s32[128,6]{0,1:T(8,128)} %param.12) | copy-start | bytes 9220
  7.2 51.1 %copy-start.9 = (bf16[128,6]{0,1:T(8,128)(2,1)S(1)}, bf16[128,6]{0,1:T(8,128)(2,1)}, u32[]{:S(2)}) copy-start(bf16[128,6]{0,1:T(8,128)(2,1)} %param.13) | copy-start | bytes 4612
  7.2 90.3 %all-gather.3.cloned.1.call-start = ((), (), s32[]{:S(2)}) async-start(), calls=%async_computation.6 | async-start | bytes 4128768 | tf_op jit(solution)/shard_map/all_gather | solution.py:41
  8.4 50.1 %copy-start.7 = (bf16[128,256]{1,0:T(8,128)(2,1)S(1)}, bf16[128,256]{1,0:T(8,128)(2,1)}, u32[]{:S(2)}) copy-start(bf16[128,256]{1,0:T(8,128)(2,1)} %param.11) | copy-start | bytes 196612
  58.2 81.4 %all-gather.5.cloned.1.call-start = ((), (), s32[]{:S(2)}) async-start(), calls=%async_computation.8 | async-start | bytes 4128768 | tf_op jit(solution)/shard_map/all_gather | solution.py:42
  96.5 5.6 %copy-start.4 = (bf16[1,2,176,2048]{3,2,1,0:T(8,128)(2,1)S(1)}, bf16[1,2,176,2048]{3,2,1,0:T(8,128)(2,1)}, u32[]{:S(2)}) copy-start(bf16[1,2,176,2048]{3,2,1,0:T(8,128)(2,1)} %param.14) | copy-start | bytes 4325380
  97.5 94.0 %reduce-scatter.3.cloned.1.call-start = ((), (), s32[]{:S(2)}) async-start(), calls=%async_computation.7 | async-start | bytes 4128768 | tf_op jit(solution)/shard_map/reduce_scatter | solution.py:58
  97.5 4.6 %copy-start.1 = (bf16[896,2048]{1,0:T(8,128)(2,1)S(1)}, bf16[896,2048]{1,0:T(8,128)(2,1)}, u32[]{:S(2)}) copy-start(bf16[896,2048]{1,0:T(8,128)(2,1)} %all-gather.3.cloned.1.call-done) | copy-start | bytes 11010052
  147.2 91.1 %reduce-scatter.5.cloned.1.call-start = ((), (), s32[]{:S(2)}) async-start(), calls=%async_computation.9 | async-start | bytes 4128768 | tf_op jit(solution)/shard_map/reduce_scatter | solution.py:59
  147.3 1.2 copy-start.5
  151.6 104.0 %copy-start.6 = (bf16[896,176]{0,1:T(8,128)(2,1)S(1)}, bf16[896,176]{0,1:T(8,128)(2,1)}, u32[]{:S(2)}) copy-start(bf16[896,176]{0,1:T(8,128)(2,1)} %get-tuple-element.5) | copy-start | bytes 946180
  193.4 47.2 %all-to-all-start.1 = ((bf16[64,14,256]{2,1,0:T(8,128)(2,1)}), bf16[64,14,256]{2,1,0:T(8,128)(2,1)S(1)}, u32[]{:S(2)}, u32[]{:S(2)}) async-start(bf16[64,14,256]{2,1,0:T(8,128)(2,1)} %reshape.51), calls=%async_computation.2 | async-start | bytes 1048576 | tf_op jit(solution)/shard_map/all_to_all | solution.py:36
  240.6 46.7 %all-to-all-start.3 = ((bf16[64,14,256]{2,1,0:T(8,128)(2,1)}), bf16[64,14,256]{2,1,0:T(8,128)(2,1)}, u32[]{:S(2)}, u32[]{:S(2)}) async-start(bf16[64,14,256]{2,1,0:T(8,128)(2,1)} %reshape.54), calls=%async_computation.5 | async-start | bytes 1048576 | tf_op jit(solution)/shard_map/all_to_all | solution.py:36
  255.6 3.2 %copy-start.2 = (bf16[896,2048]{1,0:T(8,128)(2,1)S(1)}, bf16[896,2048]{1,0:T(8,128)(2,1)}, u32[]{:S(2)}) copy-start(bf16[896,2048]{1,0:T(8,128)(2,1)} %all-gather.3.cloned.1.call-done) | copy-start | bytes 11010052
  258.8 2.2 copy-start.3
  261.0 15.9 %copy-start.10 = (bf16[128,256]{1,0:T(8,128)(2,1)S(1)}, bf16[128,256]{1,0:T(8,128)(2,1)}, u32[]{:S(2)}) copy-start(bf16[128,256]{1,0:T(8,128)(2,1)} %param.9) | copy-start | bytes 196612
  261.0 26.4 %copy-start.11 = (bf16[128,256]{1,0:T(8,128)(2,1)S(1)}, bf16[128,256]{1,0:T(8,128)(2,1)}, u32[]{:S(2)}) copy-start(bf16[128,256]{1,0:T(8,128)(2,1)} %param.10) | copy-start | bytes 196612
Sparse Core Ops, SparseCore 0:
  58.3 36.5 all-gather.2
  97.6 42.0 all-gather.4
  147.4 44.0 reduce-scatter.2
  194.2 44.0 reduce-scatter.4

commit v2 on v1

v2 whole, which is shorter than its diff:
```python
import jax
import jax.numpy as jnp
from jax import lax
from jax.experimental import pallas as pl
from jax.experimental.pallas import tpu as pltpu
from jax.sharding import PartitionSpec as P

F32, BF16 = jnp.float32, jnp.bfloat16
X, Y, Z = 4, 4, 16
T, C, H, D, CAP, K = 128, 256, 176, 2048, 14, 8
M = 8 * CAP
G = 4 * M
RIGHT = (0, 1, 2, 3, 4, 8, 9, 10, 11)
LEFT = (0, 5, 6, 7, 12, 13, 14, 15, 11)
NT = (((1,), (1,)), ((), ()))
TN = (((0,), (0,)), ((), ()))
MESH = pl.DeviceIdType.MESH


def mm(a, b, dims=(((1,), (0,)), ((), ()))):
    return lax.dot_general(a, b, dims, preferred_element_type=F32)


def kernel(
    fh, sg, sh, fg, meta, win, wdn,
    res, car, gat, gin, gout,
    rb, cb, pu, pw, xs, ra, w, pre, hs, ht, po, pb, rl, fr, fb, ret, con, gt, zr, gb, gs,
    zsem, xsem, ysem, rsem, bsem, qsem, gsem, wsem, osem,
):
    e, t = lax.axis_index("expert"), lax.axis_index("tensor")
    x, z, y, c = e // Z, e % Z, t // 2, t % 2
    right, left = (x * Z + (z + 1) % Z, t), (x * Z + (z + Z - 1) % Z, t)
    up, down = (e, ((y + 1) % Y) * 2 + c), (e, ((y + Y - 1) % Y) * 2 + c)
    sib = (e, y * 2 + 1 - c)
    ahead = [(((x + d) % X) * Z + z, t) for d in range(X)]
    behind = [(((x + X - d) % X) * Z + z, t) for d in range(X)]
    peers = [(e, (t + r) % 8) for r in range(8)]

    loads = []
    for j in range(8):
        col = pl.multiple_of((((y + Y - j % 4) % Y) * 2 + (c + j // 4) % 2) * C, C)
        for k in range(3):
            src = win.at[k, :, pl.ds(col, C)] if k < 2 else wdn.at[:, pl.ds(col, C)]
            loads.append(pltpu.make_async_copy(src, w.at[k, j], wsem.at[k, j]))
            loads[-1].start()
    rb[0, 0:T, :] = fh[...]
    rb[0, T : T + 16, :] = meta[...]
    cb[0] = sg[...]

    barrier = pltpu.get_barrier_semaphore()
    for dev in [right, left, *ahead[1:], *peers[1:]]:
        pl.semaphore_signal(barrier, inc=1, device_id=dev, device_id_type=MESH)
    pl.semaphore_wait(barrier, 12)

    sent = []

    def send(src, dst, sems, at, dev):
        copy = pltpu.make_async_remote_copy(
            src_ref=src,
            dst_ref=dst,
            send_sem=sems.at[(0, *at)],
            recv_sem=sems.at[(1, *at)],
            device_id=dev,
            device_id_type=MESH,
        )
        copy.start()
        sent.append(copy)
        return copy

    zcopy = {}
    zlast = {(0, 0): 8, (0, 1): 7, (1, 0): 7, (1, 1): 8}

    def zstep(s):
        for a in range(2):
            buf = (rb, cb)[a]
            for d in range(2):
                place = (RIGHT, LEFT)[d]
                if s > 1 and s - 1 <= zlast[a, d]:
                    zcopy[a, d, s - 1].wait_recv()
                if s <= zlast[a, d]:
                    zcopy[a, d, s] = send(
                        buf.at[place[s - 1]], buf.at[place[s]], zsem, (a, place[s]), (right, left)[d]
                    )

    before = lax.broadcasted_iota(jnp.int32, (T, T), 0) < lax.broadcasted_iota(jnp.int32, (T, T), 1)
    before = jnp.where(before, 1.0, 0.0).astype(BF16)

    def experts(d):
        return (((x + d) % X) * Z + z).astype(F32)

    def slots(g):
        ids = rb[8 * g : 8 * g + 8, T : T + 16, 0:128].astype(F32)
        gates = rb[8 * g : 8 * g + 8, T : T + 16, 128:256].astype(F32)
        member, weight = [], []
        for d in range(X):
            hit = ids == experts(d)
            member.append(jnp.sum(jnp.where(hit, 1.0, 0.0), axis=1))
            weight.append(jnp.sum(jnp.where(hit, gates, 0.0), axis=1))
        member, weight = jnp.concatenate(member, axis=0), jnp.concatenate(weight, axis=0)
        rank = mm(member.astype(BF16), before)
        source = lax.broadcasted_iota(jnp.int32, (32, T), 0) % 8
        place = jnp.where(member > 0.5, rank + (CAP * source).astype(F32), -1.0)
        row = lax.broadcasted_iota(jnp.int32, (M, T), 0).astype(F32)
        for d in range(X):
            for i in range(8):
                n = 8 * d + i
                here = row == place[n : n + 1, :]
                pu[g, M * d : M * d + M, T * i : T * i + T] = jnp.where(here, 1.0, 0.0).astype(BF16)
                pw[g, M * d : M * d + M, T * i : T * i + T] = jnp.where(
                    here, jnp.broadcast_to(weight[n : n + 1, :], (M, T)), 0.0
                ).astype(BF16)

    xcopy = {}

    def xsend(a, g):
        if a == 0:
            chosen = mm(pu[g], rb[8 * g : 8 * g + 8, 0:T, :].reshape(8 * T, C))
        else:
            chosen = mm(pw[g], cb[8 * g : 8 * g + 8].reshape(8 * T, C))
        chosen = chosen.astype(BF16).reshape(X, M, C)
        xs[a, g] = chosen
        ra[a, 0, 4 * g] = chosen[0]
        for d in range(1, X):
            xcopy[a, g, d] = send(
                xs.at[a, g, d], ra.at[a, 0, 4 * g + d], xsem, (a, g, d - 1), ahead[d]
            )

    ycopy = {}

    def ysend(a, g):
        for d in range(1, X):
            xcopy[a, g, d].wait_recv()
        own = ra.at[a, 0, pl.ds(4 * g, 4)]
        for n, (j, dev) in enumerate(((1, up), (3, down), (4, sib))):
            ycopy[a, g, n] = send(own, ra.at[a, j, pl.ds(4 * g, 4)], ysem, (a, g, n), dev)

    def yforward(a, g):
        for n, j, at, dev in ((0, 1, 0, up), (1, 3, 2, down)):
            ycopy[a, g, n].wait_recv()
            half = pl.ds(4 * g + at, 2)
            ycopy[a, g, 3 + n] = send(ra.at[a, j, half], ra.at[a, 2, half], ysem, (a, g, 3 + n), dev)
            whole = pl.ds(4 * g, 4)
            ycopy[a, g, 4 + j] = send(
                ra.at[a, j, whole], ra.at[a, 4 + j, whole], ysem, (a, g, 4 + j), sib
            )

    def yfinish(a, g):
        ycopy[a, g, 3].wait_recv()
        ycopy[a, g, 4].wait_recv()
        whole = pl.ds(4 * g, 4)
        ycopy[a, g, 6] = send(ra.at[a, 2, whole], ra.at[a, 6, whole], ysem, (a, g, 6), sib)

    def yall(a, g):
        for n in (2, 5, 6, 7):
            ycopy[a, g, n].wait_recv()

    def block(ref, a, j, g):
        return ref[a, j, 4 * g : 4 * g + 4].reshape(G, C)

    def first(g):
        for k, a in ((0, 0), (1, 0), (2, 1)):
            for half in range(2):
                js = range(4 * half, 4 * half + 4)
                rows = jnp.concatenate([block(ra, a, j, g) for j in js], axis=1)
                part = mm(rows, jnp.concatenate([w[k, j] for j in js], axis=1), NT)
                pre[k] = part if half == 0 else pre[k] + part

        def gates(i, _):
            at = pl.ds(pl.multiple_of(i * M, 8), M)
            gate_pre, up_pre, hidden_grad = pre[0, at, :], pre[1, at, :], pre[2, at, :]
            sigma = jax.nn.sigmoid(gate_pre)
            active = gate_pre * sigma
            slope = hidden_grad * up_pre * sigma * (1.0 + gate_pre * (1.0 - sigma))
            for k, value in enumerate((active * up_pre, slope, hidden_grad * active)):
                hs[k, 4 * g + i, :, 0:H] = value.astype(BF16)
            return 0

        lax.fori_loop(0, 4, gates, 0)

    rcopy = {}

    def pieces(a, g):
        def one(j, _):
            if a == 0:
                part = mm(hs[0, 4 * g : 4 * g + 4].reshape(G, C)[:, 0:H], w[2, j])
            else:
                part = mm(hs[1, 4 * g : 4 * g + 4].reshape(G, C)[:, 0:H], w[0, j])
                part += mm(hs[2, 4 * g : 4 * g + 4].reshape(G, C)[:, 0:H], w[1, j])
            po[a, g, j] = part.astype(BF16).reshape(X, M, C)
            return 0

        lax.fori_loop(0, 8, one, 0)
        for n in (2, 1, 3, 0):
            rcopy[a, g, n] = send(po.at[a, g, 4 + n], pb.at[a, g, n], rsem, (a, g, n), sib)

    def total(a, g, n):
        rcopy[a, g, n].wait_recv()

        def one(i, _):
            po[a, g, n, i] = (po[a, g, n, i].astype(F32) + pb[a, g, n, i].astype(F32)).astype(BF16)
            return 0

        lax.fori_loop(0, 4, one, 0)

    def reduce_far(a, g):
        total(a, g, 2)
        for n, dev in ((0, down), (1, up)):
            rcopy[a, g, 4 + n] = send(
                po.at[a, g, 2, pl.ds(2 * n, 2)], rl.at[a, g, n], rsem, (a, g, 4 + n), dev
            )

    def reduce_near(a, g):
        for n, j, dev in ((0, 1, down), (1, 3, up)):
            total(a, g, j)
            rcopy[a, g, 4 + n].wait_recv()
            for i in range(2):
                po[a, g, j, 2 * n + i] = (
                    po[a, g, j, 2 * n + i].astype(F32) + rl[a, g, n, i].astype(F32)
                ).astype(BF16)
            rcopy[a, g, 6 + n] = send(po.at[a, g, j], fr.at[a, g, n], rsem, (a, g, 6 + n), dev)

    bcopy = {}

    def give_back(a, g):
        for n in (0, 6, 7):
            rcopy[a, g, n].wait_recv()

        def one(i, _):
            fb[a, g, i] = (
                po[a, g, 0, i].astype(F32)
                + pb[a, g, 0, i].astype(F32)
                + fr[a, g, 0, i].astype(F32)
                + fr[a, g, 1, i].astype(F32)
            ).astype(BF16)
            return 0

        lax.fori_loop(0, 4, one, 0)
        ret[a, g, 0] = fb[a, g, 0]
        for d in range(1, X):
            bcopy[a, g, d] = send(fb.at[a, g, d], ret.at[a, g, d], bsem, (a, g, d - 1), behind[d])

    def combine(a, g):
        for d in range(1, X):
            bcopy[a, g, d].wait_recv()
        rows = ret[a, g].reshape(G, C)
        table = (pw, pu)[a]
        for i in range(8):
            con[a, 8 * g + i] = mm(table[g, :, T * i : T * i + T], rows, TN)
        if a == 0:
            dots = jnp.sum(
                xs[1, g].reshape(G, C).astype(F32) * rows.astype(F32), axis=1, keepdims=True
            )
            for i in range(8):
                spread = pu[g, :, T * i : T * i + T].astype(F32) * dots
                ids = rb[8 * g + i, T : T + 16, 0:128].astype(F32)
                gates = rb[8 * g + i, T : T + 16, 128:256].astype(F32)
                parts = jnp.zeros((16, T), F32)
                for d in range(X):
                    line = jnp.sum(spread[M * d : M * d + M], axis=0, keepdims=True)
                    parts += jnp.where(ids == experts(d), line, 0.0)
                gt[8 * g + i] = parts / gates

    qcopy = {}
    qfirst = {(0, 0): 7, (0, 1): 8, (1, 0): 8, (1, 1): 7}

    def qsend(a, d, s):
        rows = pl.ds(0, T + 16 if a == 0 else T)
        qcopy[a, d, s] = send(
            zr.at[a, d, s, rows], zr.at[a, d, s - 1, rows], qsem, (a, d, s - 1), (right, left)[d]
        )

    def qstart(a):
        for d in range(2):
            s = qfirst[a, d]
            place = (LEFT, RIGHT)[d][s]
            zr[a, d, s, 0:T] = con[a, place].astype(BF16)
            if a == 0:
                zr[a, d, s, T : T + 16, 0:128] = gt[place].astype(BF16)
                zr[a, d, s, T : T + 16, 128:256] = jnp.zeros((16, 128), BF16)
            qsend(a, d, s)

    def qstep(a, back):
        for d in range(2):
            s = qfirst[a, d] - back
            if s < 0:
                continue
            qcopy[a, d, s + 1].wait_recv()
            if s == 0:
                continue
            place = (LEFT, RIGHT)[d][s]
            zr[a, d, s, 0:T] = (zr[a, d, s, 0:T].astype(F32) + con[a, place]).astype(BF16)
            if a == 0:
                zr[a, d, s, T : T + 16, 0:128] = (
                    zr[a, d, s, T : T + 16, 0:128].astype(F32) + gt[place]
                ).astype(BF16)
            qsend(a, d, s)

    def weight_grads():
        for k in range(3):
            ht[k] = jnp.transpose(hs[k].reshape(2 * G, C))

        def one(j, _):
            for k, n, a in ((0, 1, 0), (1, 2, 0), (2, 0, 1)):
                gs[k, j] = mm(ht[n, 0:H, :], ra[a, j].reshape(2 * G, C)).astype(BF16)
            return 0

        lax.fori_loop(0, 8, one, 0)
        for j in range(8):
            col = pl.multiple_of((((y + Y - j % 4) % Y) * 2 + (c + j // 4) % 2) * C, C)
            for k in range(3):
                dst = gin.at[k, :, pl.ds(col, C)] if k < 2 else gout.at[:, pl.ds(col, C)]
                sent_local.append(pltpu.make_async_copy(gs.at[k, j], dst, osem.at[k, j]))
                sent_local[-1].start()

    sent_local = []

    zstep(1)
    hs[:, :, :, 128:256] = jnp.zeros((3, 8, M, 128), BF16)
    for s in (2, 3, 4, 5):
        zstep(s)
    slots(0)
    xsend(0, 0)
    xsend(1, 0)
    zstep(6)
    ysend(0, 0)
    ysend(1, 0)
    zstep(7)
    yforward(0, 0)
    zstep(8)
    yforward(1, 0)
    for load in loads:
        load.wait()
    zstep(9)
    slots(1)
    xsend(0, 1)
    xsend(1, 1)
    yfinish(0, 0)
    ysend(0, 1)
    yfinish(1, 0)
    ysend(1, 1)
    yall(0, 0)
    yall(1, 0)
    first(0)
    yforward(0, 1)
    pieces(0, 0)
    yforward(1, 1)
    yfinish(0, 1)
    pieces(1, 0)
    reduce_far(0, 0)
    yfinish(1, 1)
    yall(0, 1)
    yall(1, 1)
    first(1)
    pieces(0, 1)
    reduce_near(0, 0)
    reduce_far(0, 1)
    reduce_far(1, 0)
    pieces(1, 1)
    reduce_near(0, 1)
    give_back(0, 0)
    reduce_near(1, 0)
    reduce_far(1, 1)
    give_back(0, 1)
    combine(0, 0)
    give_back(1, 0)
    reduce_near(1, 1)
    combine(0, 1)
    qstart(0)
    weight_grads()
    qstep(0, 1)
    give_back(1, 1)
    combine(1, 0)
    qstep(0, 2)
    combine(1, 1)
    qstart(1)
    for back in range(3, 9):
        qstep(0, back)
        qstep(1, back - 2)

    here = gt[0] + zr[0, 0, 0, T : T + 16, 0:128].astype(F32) + zr[0, 1, 0, T : T + 16, 0:128].astype(F32)
    gb[0] = here[0:8]
    gcopy = [send(gb.at[0], gb.at[r], gsem, (r - 1,), peers[r]) for r in range(1, 8)]
    branch = con[0, 0] + zr[0, 0, 0, 0:T].astype(F32) + zr[0, 1, 0, 0:T].astype(F32)
    res[...] = (sh[...].astype(F32) - branch).astype(BF16)
    for copy in gcopy:
        copy.wait_recv()
    gat[...] = sum(gb[r] for r in range(8))
    qstep(1, 7)
    qstep(1, 8)
    branch = con[1, 0] + zr[1, 0, 0, 0:T].astype(F32) + zr[1, 1, 0, 0:T].astype(F32)
    car[...] = (fg[...].astype(F32) + branch).astype(BF16)
    for copy in sent:
        copy.wait_send()
    for copy in sent_local:
        copy.wait()


def body(first_half, second_half, first_grad, second_grad, expert_ids, gate_weights, expert_in, expert_out):
    ids = jnp.pad(expert_ids.T.astype(BF16), ((0, 10), (0, 0)), constant_values=-1)
    gates = jnp.pad(gate_weights.T, ((0, 10), (0, 0)), constant_values=1)
    meta = jnp.concatenate([ids, gates], axis=1)
    vmem, hbm = pl.BlockSpec(memory_space=pltpu.VMEM), pl.BlockSpec(memory_space=pl.ANY)
    dma = pltpu.SemaphoreType.DMA
    shape = jax.ShapeDtypeStruct
    res, car, gat, gin, gout = pl.pallas_call(
        kernel,
        out_shape=(
            shape((T, C), BF16),
            shape((T, C), BF16),
            shape((8, T), F32),
            shape((2, H, D), BF16),
            shape((H, D), BF16),
        ),
        in_specs=[vmem] * 5 + [hbm] * 2,
        out_specs=(vmem, vmem, vmem, hbm, hbm),
        scratch_shapes=[
            pltpu.VMEM((16, T + 16, C), BF16),
            pltpu.VMEM((16, T, C), BF16),
            pltpu.VMEM((2, G, 8 * T), BF16),
            pltpu.VMEM((2, G, 8 * T), BF16),
            pltpu.VMEM((2, 2, X, M, C), BF16),
            pltpu.VMEM((2, 8, 8, M, C), BF16),
            pltpu.VMEM((3, 8, H, C), BF16),
            pltpu.VMEM((3, G, H), F32),
            pltpu.VMEM((3, 8, M, C), BF16),
            pltpu.VMEM((3, C, 2 * G), BF16),
            pltpu.VMEM((2, 2, 8, X, M, C), BF16),
            pltpu.VMEM((2, 2, 4, X, M, C), BF16),
            pltpu.VMEM((2, 2, 2, 2, M, C), BF16),
            pltpu.VMEM((2, 2, 2, X, M, C), BF16),
            pltpu.VMEM((2, 2, X, M, C), BF16),
            pltpu.VMEM((2, 2, X, M, C), BF16),
            pltpu.VMEM((2, 16, T, C), F32),
            pltpu.VMEM((16, 16, T), F32),
            pltpu.VMEM((2, 2, 9, T + 16, C), BF16),
            pltpu.VMEM((8, 8, T), F32),
            pltpu.VMEM((3, 8, H, C), BF16),
            dma((2, 2, 16)),
            dma((2, 2, 2, 3)),
            dma((2, 2, 2, 8)),
            dma((2, 2, 2, 8)),
            dma((2, 2, 2, 3)),
            dma((2, 2, 2, 8)),
            dma((2, 7)),
            dma((3, 8)),
            dma((3, 8)),
        ],
        compiler_params=pltpu.CompilerParams(
            collective_id=0, has_side_effects=True, vmem_limit_bytes=58 * 2**20
        ),
    )(first_half, second_grad, second_half, first_grad, meta, expert_in[0], expert_out[0])
    return res, car, gat[0:6].T, gin[None], gout[None]


def solution(mesh):
    tokens = P("expert", "tensor")
    routes = P("expert", None)
    weights = (P("expert", None, "tensor", None), P("expert", "tensor", None))
    return jax.shard_map(
        body,
        mesh=mesh,
        in_specs=(tokens, tokens, tokens, tokens, routes, routes, *weights),
        out_specs=(tokens, tokens, routes, *weights),
        check_vma=False,
    )
```

time: 296 us -> 157 us (0.53)
  the two profiles are of different devices: /device:TPU:31 before, /device:TPU:1 now
where the time goes in v2:
time: 157 us; the launch traced here: 156 us
  Pallas kernels  146 us (93%)
  local copies, waits for them, and re-layouts  7.77 us (5%)
  other arithmetic  1.97 us (1%)
    pallas_call x1, Pallas kernels, body(): pl.pallas_call(kernel, out_shape=(shape((T, C), BF16), shape((T, C), BF16...  146 us
    unnamed x6, local copies, waits for them, and re-layouts  6.5 us

profile of v2, /device:TPU:1, one launch (start us, length us, event | category | flops | bytes accessed | tf_op | source)
XLA Modules:
  0.0 156.3 jit_solution(4766289237657208397)
XLA Ops:
  0.6 0.7 convert_bitcast_fusion
  1.3 1.3 fusion.2.meta
  2.6 145.9 %shard_map.119 = (bf16[128,256]{1,0:T(8,128)(2,1)}, bf16[128,256]{1,0:T(8,128)(2,1)}, f32[8,128]{1,0:T(8,128)}, bf16[2,176,2048]{2,1,0:T(8,128)(2,1)}, bf16[176,2048]{1,0:T(8,128)(2,1)}) custom-call(bf16[128,256]{1,0:T(8,128)(2,1)} %fh.1, bf16[128,256]{1,0:T(8,128)(2,1)} %sg.1, bf16[128,256]{1,0:T(8,128)(2,1)} %sh.1, bf16[128,256]{1,0:T(8,128)(2,1)} %fg.1, ...), custom_call_target="tpu_custom_call" | custom-call | tf_op jit(solution)/shard_map/pallas_call | solution.py:405
  148.6 1.3 slice_bitcast_fusion
  149.8 1.5 copy.17
  151.3 1.5 copy.18
  152.8 0.0 copy-start
  152.8 2.7 %copy.19 = bf16[1,2,176,2048]{3,2,1,0:T(8,128)(2,1)} copy(bf16[1,2,176,2048]{3,2,1,0:T(8,128)(2,1)} %bitcast.10) | data formatting | bytes 2883584
  155.5 0.0 copy-done
  155.5 0.9 copy.20
Async XLA Ops:
  152.8 2.7 %copy-start = (bf16[176,2048]{1,0:T(8,128)(2,1)S(1)}, bf16[176,2048]{1,0:T(8,128)(2,1)}, u32[]{:S(2)}) copy-start(bf16[176,2048]{1,0:T(8,128)(2,1)} %get-tuple-element.14) | copy-start | bytes 2162692

commit v3 on v2

--- a/solution.py
+++ b/solution.py
@@ -22,7 +22,7 @@
 
 
 def kernel(
-    fh, sg, sh, fg, meta, win, wdn,
+    fh, sg, sh, fg, ids, gates, win, wdn,
     res, car, gat, gin, gout,
     rb, cb, pu, pw, xs, ra, w, pre, hs, ht, po, pb, rl, fr, fb, ret, con, gt, zr, gb, gs,
     zsem, xsem, ysem, rsem, bsem, qsem, gsem, wsem, osem,
@@ -44,7 +44,10 @@
             loads.append(pltpu.make_async_copy(src, w.at[k, j], wsem.at[k, j]))
             loads[-1].start()
     rb[0, 0:T, :] = fh[...]
-    rb[0, T : T + 16, :] = meta[...]
+    blank = jnp.ones((10, T), F32)
+    names = jnp.concatenate([ids[...].astype(F32), -blank], axis=0)
+    rb[0, T : T + 16, 0:128] = names.astype(BF16)
+    rb[0, T : T + 16, 128:256] = jnp.concatenate([gates[...].astype(F32), blank], axis=0).astype(BF16)
     cb[0] = sg[...]
 
     barrier = pltpu.get_barrier_semaphore()
@@ -165,7 +168,7 @@
                 part = mm(rows, jnp.concatenate([w[k, j] for j in js], axis=1), NT)
                 pre[k] = part if half == 0 else pre[k] + part
 
-        def gates(i, _):
+        def gated(i, _):
             at = pl.ds(pl.multiple_of(i * M, 8), M)
             gate_pre, up_pre, hidden_grad = pre[0, at, :], pre[1, at, :], pre[2, at, :]
             sigma = jax.nn.sigmoid(gate_pre)
@@ -175,7 +178,7 @@
                 hs[k, 4 * g + i, :, 0:H] = value.astype(BF16)
             return 0
 
-        lax.fori_loop(0, 4, gates, 0)
+        lax.fori_loop(0, 4, gated, 0)
 
     rcopy = {}
 
@@ -246,19 +249,21 @@
         table = (pw, pu)[a]
         for i in range(8):
             con[a, 8 * g + i] = mm(table[g, :, T * i : T * i + T], rows, TN)
-        if a == 0:
-            dots = jnp.sum(
-                xs[1, g].reshape(G, C).astype(F32) * rows.astype(F32), axis=1, keepdims=True
-            )
-            for i in range(8):
-                spread = pu[g, :, T * i : T * i + T].astype(F32) * dots
-                ids = rb[8 * g + i, T : T + 16, 0:128].astype(F32)
-                gates = rb[8 * g + i, T : T + 16, 128:256].astype(F32)
-                parts = jnp.zeros((16, T), F32)
-                for d in range(X):
-                    line = jnp.sum(spread[M * d : M * d + M], axis=0, keepdims=True)
-                    parts += jnp.where(ids == experts(d), line, 0.0)
-                gt[8 * g + i] = parts / gates
+
+    def gate_terms(g):
+        rows = ret[0, g].reshape(G, C)
+        dots = jnp.sum(
+            xs[1, g].reshape(G, C).astype(F32) * rows.astype(F32), axis=1, keepdims=True
+        )
+        for i in range(8):
+            spread = pu[g, :, T * i : T * i + T].astype(F32) * dots
+            ids = rb[8 * g + i, T : T + 16, 0:128].astype(F32)
+            gates = rb[8 * g + i, T : T + 16, 128:256].astype(F32)
+            parts = jnp.zeros((16, T), F32)
+            for d in range(X):
+                line = jnp.sum(spread[M * d : M * d + M], axis=0, keepdims=True)
+                parts += jnp.where(ids == experts(d), line, 0.0)
+            gt[8 * g + i] = parts / gates
 
     qcopy = {}
     qfirst = {(0, 0): 7, (0, 1): 8, (1, 0): 8, (1, 1): 7}
@@ -295,110 +300,154 @@
                 ).astype(BF16)
             qsend(a, d, s)
 
-    def weight_grads():
+    sent_local = []
+
+    def turn():
         for k in range(3):
             ht[k] = jnp.transpose(hs[k].reshape(2 * G, C))
 
-        def one(j, _):
-            for k, n, a in ((0, 1, 0), (1, 2, 0), (2, 0, 1)):
-                gs[k, j] = mm(ht[n, 0:H, :], ra[a, j].reshape(2 * G, C)).astype(BF16)
-            return 0
-
-        lax.fori_loop(0, 8, one, 0)
-        for j in range(8):
-            col = pl.multiple_of((((y + Y - j % 4) % Y) * 2 + (c + j // 4) % 2) * C, C)
-            for k in range(3):
-                dst = gin.at[k, :, pl.ds(col, C)] if k < 2 else gout.at[:, pl.ds(col, C)]
-                sent_local.append(pltpu.make_async_copy(gs.at[k, j], dst, osem.at[k, j]))
-                sent_local[-1].start()
-
-    sent_local = []
-
-    zstep(1)
-    hs[:, :, :, 128:256] = jnp.zeros((3, 8, M, 128), BF16)
-    for s in (2, 3, 4, 5):
-        zstep(s)
-    slots(0)
-    xsend(0, 0)
-    xsend(1, 0)
-    zstep(6)
-    ysend(0, 0)
-    ysend(1, 0)
-    zstep(7)
-    yforward(0, 0)
-    zstep(8)
-    yforward(1, 0)
-    for load in loads:
-        load.wait()
-    zstep(9)
-    slots(1)
-    xsend(0, 1)
-    xsend(1, 1)
-    yfinish(0, 0)
-    ysend(0, 1)
-    yfinish(1, 0)
-    ysend(1, 1)
-    yall(0, 0)
-    yall(1, 0)
-    first(0)
-    yforward(0, 1)
-    pieces(0, 0)
-    yforward(1, 1)
-    yfinish(0, 1)
-    pieces(1, 0)
-    reduce_far(0, 0)
-    yfinish(1, 1)
-    yall(0, 1)
-    yall(1, 1)
-    first(1)
-    pieces(0, 1)
-    reduce_near(0, 0)
-    reduce_far(0, 1)
-    reduce_far(1, 0)
-    pieces(1, 1)
-    reduce_near(0, 1)
-    give_back(0, 0)
-    reduce_near(1, 0)
-    reduce_far(1, 1)
-    give_back(0, 1)
-    combine(0, 0)
-    give_back(1, 0)
-    reduce_near(1, 1)
-    combine(0, 1)
-    qstart(0)
-    weight_grads()
-    qstep(0, 1)
-    give_back(1, 1)
-    combine(1, 0)
-    qstep(0, 2)
-    combine(1, 1)
-    qstart(1)
-    for back in range(3, 9):
-        qstep(0, back)
-        qstep(1, back - 2)
-
-    here = gt[0] + zr[0, 0, 0, T : T + 16, 0:128].astype(F32) + zr[0, 1, 0, T : T + 16, 0:128].astype(F32)
-    gb[0] = here[0:8]
-    gcopy = [send(gb.at[0], gb.at[r], gsem, (r - 1,), peers[r]) for r in range(1, 8)]
-    branch = con[0, 0] + zr[0, 0, 0, 0:T].astype(F32) + zr[0, 1, 0, 0:T].astype(F32)
-    res[...] = (sh[...].astype(F32) - branch).astype(BF16)
-    for copy in gcopy:
-        copy.wait_recv()
-    gat[...] = sum(gb[r] for r in range(8))
-    qstep(1, 7)
-    qstep(1, 8)
-    branch = con[1, 0] + zr[1, 0, 0, 0:T].astype(F32) + zr[1, 1, 0, 0:T].astype(F32)
-    car[...] = (fg[...].astype(F32) + branch).astype(BF16)
+    def weight_grads(j):
+        col = pl.multiple_of((((y + Y - j % 4) % Y) * 2 + (c + j // 4) % 2) * C, C)
+        for k, n, a in ((0, 1, 0), (1, 2, 0), (2, 0, 1)):
+            gs[k, j] = mm(ht[n, 0:H, :], ra[a, j].reshape(2 * G, C)).astype(BF16)
+            dst = gin.at[k, :, pl.ds(col, C)] if k < 2 else gout.at[:, pl.ds(col, C)]
+            sent_local.append(pltpu.make_async_copy(gs.at[k, j], dst, osem.at[k, j]))
+            sent_local[-1].start()
+
+    def prepare():
+        hs[:, :, :, 128:256] = jnp.zeros((3, 8, M, 128), BF16)
+
+    def loaded():
+        for load in loads:
+            load.wait()
+
+    gcopy = {}
+
+    def finish(a):
+        branch = con[a, 0] + zr[a, 0, 0, 0:T].astype(F32) + zr[a, 1, 0, 0:T].astype(F32)
+        if a == 0:
+            lines = slice(T, T + 16)
+            here = gt[0] + zr[0, 0, 0, lines, 0:128].astype(F32) + zr[0, 1, 0, lines, 0:128].astype(F32)
+            gb[0] = here[0:8]
+            for r in range(1, 8):
+                gcopy[r] = send(gb.at[0], gb.at[r], gsem, (r - 1,), peers[r])
+            res[...] = (sh[...].astype(F32) - branch).astype(BF16)
+        else:
+            car[...] = (fg[...].astype(F32) + branch).astype(BF16)
+
+    def gate_total():
+        for r in range(1, 8):
+            gcopy[r].wait_recv()
+        gat[...] = sum(gb[r] for r in range(8))
+
+    steps = [
+        (zstep, 1),
+        (prepare,),
+        (zstep, 2),
+        (zstep, 3),
+        (zstep, 4),
+        (zstep, 5),
+        (slots, 0),
+        (xsend, 0, 0),
+        (xsend, 1, 0),
+        (zstep, 6),
+        (ysend, 0, 0),
+        (ysend, 1, 0),
+        (zstep, 7),
+        (yforward, 0, 0),
+        (zstep, 8),
+        (yforward, 1, 0),
+        (loaded,),
+        (zstep, 9),
+        (slots, 1),
+        (xsend, 0, 1),
+        (xsend, 1, 1),
+        (yfinish, 0, 0),
+        (ysend, 0, 1),
+        (yfinish, 1, 0),
+        (ysend, 1, 1),
+        (yall, 0, 0),
+        (yall, 1, 0),
+        (first, 0),
+        (yforward, 0, 1),
+        (pieces, 0, 0),
+        (yforward, 1, 1),
+        (reduce_far, 0, 0),
+        (yfinish, 0, 1),
+        (pieces, 1, 0),
+        (yfinish, 1, 1),
+        (reduce_near, 0, 0),
+        (yall, 0, 1),
+        (reduce_far, 1, 0),
+        (yall, 1, 1),
+        (first, 1),
+        (pieces, 0, 1),
+        (reduce_near, 1, 0),
+        (reduce_far, 0, 1),
+        (give_back, 0, 0),
+        (pieces, 1, 1),
+        (reduce_near, 0, 1),
+        (reduce_far, 1, 1),
+        (give_back, 1, 0),
+        (turn,),
+        (combine, 0, 0),
+        (give_back, 0, 1),
+        (reduce_near, 1, 1),
+        (gate_terms, 0),
+        (combine, 0, 1),
+        (gate_terms, 1),
+        (qstart, 0),
+        (combine, 1, 0),
+        (give_back, 1, 1),
+        (qstep, 0, 1),
+        (weight_grads, 0),
+        (combine, 1, 1),
+        (qstart, 1),
+        (qstep, 0, 2),
+        (weight_grads, 1),
+        (qstep, 1, 1),
+        (qstep, 0, 3),
+        (weight_grads, 2),
+        (qstep, 1, 2),
+        (qstep, 0, 4),
+        (weight_grads, 3),
+        (qstep, 1, 3),
+        (qstep, 0, 5),
+        (weight_grads, 4),
+        (qstep, 1, 4),
+        (qstep, 0, 6),
+        (weight_grads, 5),
+        (qstep, 1, 5),
+        (qstep, 0, 7),
+        (weight_grads, 6),
+        (qstep, 1, 6),
+        (qstep, 0, 8),
+        (finish, 0),
+        (weight_grads, 7),
+        (qstep, 1, 7),
+        (gate_total,),
+        (qstep, 1, 8),
+        (finish, 1),
+    ]
+    for step, *at in steps:
+        step(*at)
     for copy in sent:
         copy.wait_send()
     for copy in sent_local:
         copy.wait()
 
 
+def settle(res, car, gat, gin, gout, res_out, car_out, gat_out, gin_out, gout_out, sem):
+    pairs = ((gin, gin_out), (gout, gout_out), (res, res_out), (car, car_out))
+    copies = [pltpu.make_async_copy(src, dst, sem.at[n]) for n, (src, dst) in enumerate(pairs)]
+    for copy in copies:
+        copy.start()
+    gat_out[...] = gat[0:6]
+    for copy in copies:
+        copy.wait()
+
+
 def body(first_half, second_half, first_grad, second_grad, expert_ids, gate_weights, expert_in, expert_out):
-    ids = jnp.pad(expert_ids.T.astype(BF16), ((0, 10), (0, 0)), constant_values=-1)
-    gates = jnp.pad(gate_weights.T, ((0, 10), (0, 0)), constant_values=1)
-    meta = jnp.concatenate([ids, gates], axis=1)
     vmem, hbm = pl.BlockSpec(memory_space=pltpu.VMEM), pl.BlockSpec(memory_space=pl.ANY)
     dma = pltpu.SemaphoreType.DMA
     shape = jax.ShapeDtypeStruct
@@ -411,7 +460,7 @@
             shape((2, H, D), BF16),
             shape((H, D), BF16),
         ),
-        in_specs=[vmem] * 5 + [hbm] * 2,
+        in_specs=[vmem] * 6 + [hbm] * 2,
         out_specs=(vmem, vmem, vmem, hbm, hbm),
         scratch_shapes=[
             pltpu.VMEM((16, T + 16, C), BF16),
@@ -448,8 +497,21 @@
         compiler_params=pltpu.CompilerParams(
             collective_id=0, has_side_effects=True, vmem_limit_bytes=58 * 2**20
         ),
-    )(first_half, second_grad, second_half, first_grad, meta, expert_in[0], expert_out[0])
-    return res, car, gat[0:6].T, gin[None], gout[None]
+    )(first_half, second_grad, second_half, first_grad, expert_ids.T, gate_weights.T, expert_in[0], expert_out[0])
+    res, car, gat, gin, gout = pl.pallas_call(
+        settle,
+        out_shape=(
+            shape((T, C), BF16),
+            shape((T, C), BF16),
+            shape((6, T), F32),
+            shape((2, H, D), BF16),
+            shape((H, D), BF16),
+        ),
+        in_specs=[vmem] * 5,
+        out_specs=(hbm, hbm, vmem, hbm, hbm),
+        scratch_shapes=[dma((4,))],
+    )(res, car, gat, gin, gout)
+    return res, car, gat.T, gin[None], gout[None]
 
 
 def solution(mesh):

time: 157 us -> 143 us (0.911)
  local copies, waits for them, and re-layouts: 7.77 us -> 0 us
  Pallas kernels: 146 us -> 141 us
  other arithmetic: 1.97 us -> 0 us
    pallas_call x1, Pallas kernels: 146 us -> 137 us  [body(): pl.pallas_call(kernel, out_shape=(shape((T, C), BF16), shape((T, C), BF16...]
    unnamed x6 -> x0, local copies, waits for them, and re-layouts: 6.5 us -> none
    pallas_call x0 -> x1, Pallas kernels: none -> 3.6 us  [body(): pl.pallas_call(settle, out_shape=(shape((T, C), BF16), shape((T, C), BF16...]
where the time goes in v3:
time: 143 us; the launch traced here: 142 us
  Pallas kernels  141 us (99%)
    pallas_call x1, Pallas kernels, body(): pl.pallas_call(kernel, out_shape=(shape((T, C), BF16), shape((T, C), BF16...  137 us
    pallas_call x1, Pallas kernels, body(): pl.pallas_call(settle, out_shape=(shape((T, C), BF16), shape((T, C), BF16...  3.6 us

profile of v3, /device:TPU:1, one launch (start us, length us, event | category | flops | bytes accessed | tf_op | source)
XLA Modules:
  0.0 141.8 jit_solution(4922894543008494533)
XLA Ops:
  0.6 137.4 %shard_map.119 = (bf16[128,256]{1,0:T(8,128)(2,1)}, bf16[128,256]{1,0:T(8,128)(2,1)}, f32[8,128]{1,0:T(8,128)}, bf16[2,176,2048]{2,1,0:T(8,128)(2,1)}, bf16[176,2048]{1,0:T(8,128)(2,1)}) custom-call(bf16[128,256]{1,0:T(8,128)(2,1)} %fh.1, bf16[128,256]{1,0:T(8,128)(2,1)} %sg.1, bf16[128,256]{1,0:T(8,128)(2,1)} %sh.1, bf16[128,256]{1,0:T(8,128)(2,1)} %fg.1, ...), custom_call_target="tpu_custom_call" | custom-call | tf_op jit(solution)/shard_map/pallas_call | solution.py:454
  138.0 3.6 %shard_map.120 = (bf16[128,256]{1,0:T(8,128)(2,1)}, bf16[128,256]{1,0:T(8,128)(2,1)}, f32[6,128]{1,0:T(8,128)}, bf16[2,176,2048]{2,1,0:T(8,128)(2,1)}, bf16[176,2048]{1,0:T(8,128)(2,1)}) custom-call(bf16[128,256]{1,0:T(8,128)(2,1)} %get-tuple-element.15.res, bf16[128,256]{1,0:T(8,128)(2,1)} %get-tuple-element.16.car, f32[8,128]{1,0:T(8,128)} %get-tuple-element.17.gat, ...), custom_call_target="tpu_custom_call" | custom-call | tf_op jit(solution)/shard_map/pallas_call | solution.py:501

commit v4 on v3

--- a/solution.py
+++ b/solution.py
@@ -268,37 +268,39 @@
     qcopy = {}
     qfirst = {(0, 0): 7, (0, 1): 8, (1, 0): 8, (1, 1): 7}
 
-    def qsend(a, d, s):
-        rows = pl.ds(0, T + 16 if a == 0 else T)
-        qcopy[a, d, s] = send(
-            zr.at[a, d, s, rows], zr.at[a, d, s - 1, rows], qsem, (a, d, s - 1), (right, left)[d]
+    def qsend(a, d, h, s):
+        rows = pl.ds(T // 2 * h, T // 2 + (16 if h == 1 and a == 0 else 0))
+        qcopy[a, d, h, s] = send(
+            zr.at[a, d, s, rows], zr.at[a, d, s - 1, rows], qsem, (a, d, h, s - 1), (right, left)[d]
         )
 
     def qstart(a):
-        for d in range(2):
+        for h, d in ((0, 0), (0, 1), (1, 0), (1, 1)):
             s = qfirst[a, d]
             place = (LEFT, RIGHT)[d][s]
-            zr[a, d, s, 0:T] = con[a, place].astype(BF16)
-            if a == 0:
+            rows = slice(T // 2 * h, T // 2 * h + T // 2)
+            zr[a, d, s, rows] = con[a, place, rows].astype(BF16)
+            if a == 0 and h == 1:
                 zr[a, d, s, T : T + 16, 0:128] = gt[place].astype(BF16)
                 zr[a, d, s, T : T + 16, 128:256] = jnp.zeros((16, 128), BF16)
-            qsend(a, d, s)
+            qsend(a, d, h, s)
 
     def qstep(a, back):
-        for d in range(2):
+        for h, d in ((0, 0), (0, 1), (1, 0), (1, 1)):
             s = qfirst[a, d] - back
             if s < 0:
                 continue
-            qcopy[a, d, s + 1].wait_recv()
+            qcopy[a, d, h, s + 1].wait_recv()
             if s == 0:
                 continue
             place = (LEFT, RIGHT)[d][s]
-            zr[a, d, s, 0:T] = (zr[a, d, s, 0:T].astype(F32) + con[a, place]).astype(BF16)
-            if a == 0:
+            rows = slice(T // 2 * h, T // 2 * h + T // 2)
+            zr[a, d, s, rows] = (zr[a, d, s, rows].astype(F32) + con[a, place, rows]).astype(BF16)
+            if a == 0 and h == 1:
                 zr[a, d, s, T : T + 16, 0:128] = (
                     zr[a, d, s, T : T + 16, 0:128].astype(F32) + gt[place]
                 ).astype(BF16)
-            qsend(a, d, s)
+            qsend(a, d, h, s)
 
     sent_local = []
 
@@ -352,13 +354,13 @@
         (xsend, 1, 0),
         (zstep, 6),
         (ysend, 0, 0),
+        (zstep, 7),
         (ysend, 1, 0),
-        (zstep, 7),
+        (zstep, 8),
         (yforward, 0, 0),
-        (zstep, 8),
-        (yforward, 1, 0),
         (loaded,),
         (zstep, 9),
+        (yforward, 1, 0),
         (slots, 1),
         (xsend, 0, 1),
         (xsend, 1, 1),
@@ -389,7 +391,6 @@
         (reduce_near, 0, 1),
         (reduce_far, 1, 1),
         (give_back, 1, 0),
-        (turn,),
         (combine, 0, 0),
         (give_back, 0, 1),
         (reduce_near, 1, 1),
@@ -400,9 +401,10 @@
         (combine, 1, 0),
         (give_back, 1, 1),
         (qstep, 0, 1),
-        (weight_grads, 0),
+        (turn,),
         (combine, 1, 1),
         (qstart, 1),
+        (weight_grads, 0),
         (qstep, 0, 2),
         (weight_grads, 1),
         (qstep, 1, 1),
@@ -489,7 +491,7 @@
             dma((2, 2, 2, 8)),
             dma((2, 2, 2, 8)),
             dma((2, 2, 2, 3)),
-            dma((2, 2, 2, 8)),
+            dma((2, 2, 2, 2, 8)),
             dma((2, 7)),
             dma((3, 8)),
             dma((3, 8)),

time: 143 us -> 140 us (0.979)
  Pallas kernels: 141 us -> 139 us
    pallas_call x1, Pallas kernels: 137 us -> 135 us  [body(): pl.pallas_call(kernel, out_shape=(shape((T, C), BF16), shape((T, C), BF16...]
where the time goes in v4:
time: 140 us
  Pallas kernels  139 us (99%)
    pallas_call x1, Pallas kernels, body(): pl.pallas_call(kernel, out_shape=(shape((T, C), BF16), shape((T, C), BF16...  135 us
    pallas_call x1, Pallas kernels, body(): pl.pallas_call(settle, out_shape=(shape((T, C), BF16), shape((T, C), BF16...  3.6 us

profile of v4, /device:TPU:1, one launch (start us, length us, event | category | flops | bytes accessed | tf_op | source)
XLA Modules:
  0.0 139.7 jit_solution(9092089189050378493)
XLA Ops:
  0.6 135.3 %shard_map.119 = (bf16[128,256]{1,0:T(8,128)(2,1)}, bf16[128,256]{1,0:T(8,128)(2,1)}, f32[8,128]{1,0:T(8,128)}, bf16[2,176,2048]{2,1,0:T(8,128)(2,1)}, bf16[176,2048]{1,0:T(8,128)(2,1)}) custom-call(bf16[128,256]{1,0:T(8,128)(2,1)} %fh.1, bf16[128,256]{1,0:T(8,128)(2,1)} %sg.1, bf16[128,256]{1,0:T(8,128)(2,1)} %sh.1, bf16[128,256]{1,0:T(8,128)(2,1)} %fg.1, ...), custom_call_target="tpu_custom_call" | custom-call | tf_op jit(solution)/shard_map/pallas_call | solution.py:456
  135.9 3.6 %shard_map.120 = (bf16[128,256]{1,0:T(8,128)(2,1)}, bf16[128,256]{1,0:T(8,128)(2,1)}, f32[6,128]{1,0:T(8,128)}, bf16[2,176,2048]{2,1,0:T(8,128)(2,1)}, bf16[176,2048]{1,0:T(8,128)(2,1)}) custom-call(bf16[128,256]{1,0:T(8,128)(2,1)} %get-tuple-element.15.res, bf16[128,256]{1,0:T(8,128)(2,1)} %get-tuple-element.16.car, f32[8,128]{1,0:T(8,128)} %get-tuple-element.17.gat, ...), custom_call_target="tpu_custom_call" | custom-call | tf_op jit(solution)/shard_map/pallas_call | solution.py:503
